TPU v7x, 32 devices: a whole 2x2x4 slice. The times are simulated.
32 devices in a mesh: vol: 8 (over z, y), rep: 4 (over x, core).
Axes of the slice: x: 2, y: 2, z: 4, core: 2. Of those that a mesh axis runs over, the one named last changes fastest.
Arguments:
- features: bfloat16 [8, 32, 4, 8192], P('vol', None, None, 'rep'), may hold values from -6 to 6
- deltas: float32 [8, 4, 8192], P('vol', None, 'rep'), may hold values from 0.0125 to 0.125
- counts: int32 [8, 8192], P('vol', 'rep'), may hold values from 0 to 4
- order_rank: int32 [8192, 8], P('rep'), may hold values from 0 to 7, each once within a row
- cotangent: float32 [3, 8192], P(None, 'rep'), may hold values from -6 to 6
- first_weight: bfloat16 [8, 32, 256], P('vol'), may hold values from -1.5 to 1.5
- middle_weight: bfloat16 [8, 2, 256, 256], P('vol'), may hold values from -0.5 to 0.5
- last_weight: bfloat16 [8, 256, 4], P('vol'), may hold values from -0.375 to 0.375
Outputs:
- first_grad: float32 [8, 32, 256], P('vol')
- middle_grad: float32 [8, 2, 256, 256], P('vol')
- last_grad: float32 [8, 256, 4], P('vol')
Inputs may be any that keep to these rules, and one draw needn't show every extreme that they name: `order_rank`: each ray's row holds every number of 0 .. 7 once.
All inputs are finite; a program needn't handle non-finite values.
Results may differ from a plain program's by a relative error of at most 0.0083.
Values sent between devices are 32-bit elements; how exact they have to be, the bound alone decides.
A program may use at most 128 MiB of HBM per device.

v0:
```python
import jax
import jax.numpy as jnp
from jax import lax
from jax.sharding import PartitionSpec as P


def contract_first(matrix, rows):
    return lax.dot_general(
        matrix, rows, (((0,), (0,)), ((), ())), preferred_element_type=jnp.float32
    )


def contract_last(left, right):
    return lax.dot_general(
        left, right, (((1,), (1,)), ((), ())), preferred_element_type=jnp.float32
    )


def silu_grad(pre):
    logistic = jax.nn.sigmoid(pre)
    return logistic * (1.0 + pre * (1.0 - logistic))


def forward_network(samples, first_weight, middle_weight, last_weight):
    pre = contract_first(first_weight, samples)
    preacts = [pre]
    layer_inputs = [samples]
    hidden = jax.nn.silu(pre).astype(jnp.bfloat16)
    for depth in range(middle_weight.shape[0]):
        layer_inputs.append(hidden)
        pre = contract_first(middle_weight[depth], hidden)
        preacts.append(pre)
        hidden = jax.nn.silu(pre).astype(jnp.bfloat16)
    layer_inputs.append(hidden)
    head_out = contract_first(last_weight, hidden)
    return (preacts, layer_inputs, head_out)


def render_segment(head_out, deltas, counts):
    density = jax.nn.softplus(head_out[0])
    albedo = jax.nn.sigmoid(head_out[1:])
    live = (lax.broadcasted_iota(jnp.int32, deltas.shape, 0) < counts[None, :]).astype(jnp.float32)
    optical = density * deltas * live
    reached = jnp.cumsum(optical, axis=0)
    passed = reached - optical
    leaving = jnp.exp(-reached)
    sample_weight = jnp.exp(-passed) - leaving
    colour = jnp.sum(sample_weight[None] * albedo, axis=1)
    logt = -reached[-1]
    return (colour, logt, (albedo, leaving, sample_weight, live))


def head_gradient(head_out, deltas, saved, grad_colour, grad_logt):
    albedo, leaving, sample_weight, live = saved
    facing = jnp.sum(grad_colour[:, None, :] * albedo, axis=0)
    weighted = facing * sample_weight
    later = jnp.sum(weighted, axis=0)[None] - jnp.cumsum(weighted, axis=0)
    doptical = facing * leaving - later - grad_logt[None]
    d_density = doptical * deltas * live * jax.nn.sigmoid(head_out[0])
    d_albedo = sample_weight[None] * grad_colour[:, None, :] * albedo * (1.0 - albedo)
    return jnp.concatenate([d_density[None], d_albedo], axis=0).astype(jnp.bfloat16)


def network_gradients(preacts, layer_inputs, head_grad, middle_weight, last_weight, reducers):
    last_grad = reducers[0](contract_last(layer_inputs[-1], head_grad))
    back = (
        jnp.dot(last_weight, head_grad, preferred_element_type=jnp.float32) * silu_grad(preacts[-1])
    ).astype(jnp.bfloat16)
    hidden_grads = []
    for depth in reversed(range(middle_weight.shape[0])):
        hidden_grads.append(reducers[1](contract_last(layer_inputs[depth + 1], back)))
        back = (
            jnp.dot(middle_weight[depth], back, preferred_element_type=jnp.float32)
            * silu_grad(preacts[depth])
        ).astype(jnp.bfloat16)
    first_grad = reducers[2](contract_last(layer_inputs[0], back))
    middle_grad = jnp.stack(hidden_grads[::-1], axis=0)
    return (first_grad, middle_grad, last_grad)


def composite_rays(segments, rank_rows, cotangent):
    logs = segments[:, 3]

    def add_log(index, total):
        other = lax.dynamic_index_in_dim(rank_rows, index, 0, keepdims=True)
        term = lax.dynamic_index_in_dim(logs, index, 0, keepdims=True)
        return total + jnp.where(other < rank_rows, term, 0.0)

    summed = lax.fori_loop(0, rank_rows.shape[0], add_log, jnp.zeros(rank_rows.shape, jnp.float32))
    prefix = jnp.exp(summed)
    facing = jnp.sum(cotangent[None] * segments[:, :3], axis=1) * prefix

    def add_behind(index, total):
        other = lax.dynamic_index_in_dim(rank_rows, index, 0, keepdims=True)
        term = lax.dynamic_index_in_dim(facing, index, 0, keepdims=True)
        return total + jnp.where(other > rank_rows, term, 0.0)

    behind = lax.fori_loop(
        0, rank_rows.shape[0], add_behind, jnp.zeros(rank_rows.shape, jnp.float32)
    )
    return (prefix, behind)


def unchanged(value):
    return value


def per_device(
    features, deltas, counts, order_rank, cotangent, first_weight, middle_weight, last_weight
):
    samples = features[0].reshape(features.shape[1], -1)
    preacts, layer_inputs, head_out = forward_network(
        samples, first_weight[0], middle_weight[0], last_weight[0]
    )
    shaped = head_out.reshape(4, deltas.shape[1], deltas.shape[2])
    colour, logt, saved = render_segment(shaped, deltas[0], counts[0])
    payload = jnp.concatenate([colour, logt[None]], axis=0)
    rank_rows = order_rank.T
    volumes = lax.axis_size("vol")
    mine = lax.axis_index("vol")
    share = payload.shape[1] // volumes
    outgoing = payload.reshape(1, 4, volumes, share)
    arrived = lax.all_to_all(outgoing, "vol", split_axis=2, concat_axis=0, tiled=True)[:, :, 0, :]
    rank_share = lax.dynamic_slice_in_dim(rank_rows, mine * share, share, 1)
    cot_share = lax.dynamic_slice_in_dim(cotangent, mine * share, share, 1)
    prefix, behind = composite_rays(arrived, rank_share, cot_share)
    packed = jnp.stack([prefix, behind], axis=1)[:, :, None, :]
    returned = lax.all_to_all(packed, "vol", split_axis=0, concat_axis=2, tiled=True).reshape(2, -1)
    own_prefix = returned[0]
    own_behind = returned[1]
    grad_colour = own_prefix[None] * cotangent
    head_grad = head_gradient(shaped, deltas[0], saved, grad_colour, own_behind).reshape(4, -1)
    first_grad, middle_grad, last_grad = network_gradients(
        preacts,
        layer_inputs,
        head_grad,
        middle_weight[0],
        last_weight[0],
        (unchanged, unchanged, unchanged),
    )
    first_grad, middle_grad, last_grad = lax.psum((first_grad, middle_grad, last_grad), "rep")
    return (first_grad[None], middle_grad[None], last_grad[None])


def solution(mesh):
    placed = (
        P("vol", None, None, "rep"),
        P("vol", None, "rep"),
        P("vol", "rep"),
        P("rep", None),
        P(None, "rep"),
        P("vol", None, None),
        P("vol", None, None, None),
        P("vol", None, None),
    )
    return jax.shard_map(
        per_device,
        mesh=mesh,
        in_specs=placed,
        out_specs=(P("vol", None, None), P("vol", None, None, None), P("vol", None, None)),
        check_vma=False,
    )
```

profile of v0, /device:TPU:0, one launch (start us, length us, event | category | flops | bytes accessed | tf_op | source)
XLA Modules:
  0.0 117.5 jit_solution(11876921244908839320)
XLA Ops:
  7.2 1.4 %copy.24 = bf16[4,8,4,2048]{3,1,2,0:T(8,128)(2,1)S(1)} copy(bf16[4,8,4,2048]{3,2,1,0:T(4,128)(2,1)} %bitcast.150) | data formatting | bytes 1048576
  8.6 5.5 %multiply_convert_fusion.2 = (bf16[256,8192]{1,0:T(8,128)(2,1)S(1)}, f32[256,8192]{1,0:T(8,128)}) fusion(bf16[32,8192]{1,0:T(8,128)(2,1)S(1)} %bitcast.151, bf16[1,32,256]{2,1,0:T(8,128)(2,1)} %param.17), kind=kOutput, calls=%fused_computation.22 | convolution fusion | flops 144703488 | bytes 13123584 | tf_op jit(solution)/shard_map/dot_general | solution.py:8
  14.1 4.8 %multiply_convert_fusion.1 = (bf16[256,8192]{1,0:T(8,128)(2,1)S(1)}, f32[256,8192]{1,0:T(8,128)}) fusion(bf16[256,8192]{1,0:T(8,128)(2,1)S(1)} %get-tuple-element.219, bf16[1,2,256,256]{3,2,1,0:T(8,128)(2,1)S(1)} %copy-done.6), kind=kOutput, calls=%fused_computation.20 | convolution fusion | flops 1084227584 | bytes 16908288 | tf_op jit(solution)/shard_map/dot_general | solution.py:8
  19.0 4.9 %multiply_convert_fusion = (bf16[256,8192]{1,0:T(8,128)(2,1)S(1)}, f32[256,8192]{1,0:T(8,128)}) fusion(bf16[256,8192]{1,0:T(8,128)(2,1)S(1)} %get-tuple-element.221, bf16[1,2,256,256]{3,2,1,0:T(8,128)(2,1)S(1)} %copy-done.6), kind=kOutput, calls=%fused_computation.18 | convolution fusion | flops 1084227584 | bytes 16908288 | tf_op jit(solution)/shard_map/dot_general | solution.py:8
  23.8 2.0 %copy-done.1 = bf16[256,8192]{1,0:T(8,128)(2,1)} copy-done((bf16[256,8192]{1,0:T(8,128)(2,1)}, bf16[256,8192]{1,0:T(8,128)(2,1)S(1)}, u32[]{:S(2)}) %copy-start.1) | copy-done | bytes 4194328
  25.8 0.6 convolution_bitcast_fusion.5
  27.1 0.6 pad_maximum_fusion.1
  27.7 7.3 %all-to-all-start = ((f32[1,4,8,256]{3,1,0,2:T(4,128)}), f32[1,4,8,256]{3,1,0,2:T(4,128)S(1)}, u32[]{:S(2)}, u32[]{:S(2)}) async-start(f32[1,4,8,256]{3,1,0,2:T(4,128)} %pad_maximum_fusion.1), calls=%async_computation | async-start | bytes 65536 | tf_op jit(solution)/shard_map/all_to_all | solution.py:123
  35.1 6.6 %all-to-all-done = f32[1,4,8,256]{3,1,0,2:T(4,128)S(1)} async-done(((f32[1,4,8,256]{3,1,0,2:T(4,128)}), f32[1,4,8,256]{3,1,0,2:T(4,128)S(1)}, u32[]{:S(2)}, u32[]{:S(2)}) %all-to-all-start) | async-done | bytes 32800 | tf_op jit(solution)/shard_map/all_to_all | solution.py:123
  41.8 0.5 while.28
  42.8 0.6 maximum_bitcast_fusion.1
  43.4 3.3 %all-to-all-start.1 = ((f32[8,2,1,256]{3,1,2,0:T(2,128)}), f32[8,2,1,256]{3,1,2,0:T(2,128)S(1)}, u32[]{:S(2)}, u32[]{:S(2)}) async-start(f32[8,2,1,256]{3,1,2,0:T(2,128)} %maximum_bitcast_fusion.1), calls=%async_computation.1 | async-start | bytes 32768 | tf_op jit(solution)/shard_map/all_to_all | solution.py:128
  47.0 6.3 %all-to-all-done.1 = f32[8,2,1,256]{3,1,2,0:T(2,128)S(1)} async-done(((f32[8,2,1,256]{3,1,2,0:T(2,128)}), f32[8,2,1,256]{3,1,2,0:T(2,128)S(1)}, u32[]{:S(2)}, u32[]{:S(2)}) %all-to-all-start.1) | async-done | bytes 16416 | tf_op jit(solution)/shard_map/all_to_all | solution.py:128
  53.9 5.8 %fusion.3 = bf16[256,8192]{1,0:T(8,128)(2,1)S(1)} fusion(f32[256,8192]{1,0:T(8,128)} %get-tuple-element.224, bf16[3,8192]{1,0:T(4,128)(2,1)S(1)} %get-tuple-element.212, bf16[1,8192]{1,0:T(2,128)(2,1)S(1)} %bitcast.155, bf16[1,256,4]{1,2,0:T(4,128)(2,1)S(1)} %copy-done.5), kind=kOutput, calls=%fused_computation.14 | convolution fusion | flops 35782656 | bytes 12650496 | tf_op jit(solution)/shard_map/dot_general | solution.py:67
  59.8 1.3 %convolution_bitcast_fusion.6 = f32[1,256,256]{2,1,0:T(8,128)S(1)} fusion(bf16[256,8192]{1,0:T(8,128)(2,1)S(1)} %copy-done.10, bf16[256,8192]{1,0:T(8,128)(2,1)S(1)} %fusion.3), kind=kOutput, calls=%fused_computation.25 | convolution fusion | flops 1073741824 | bytes 8650752 | tf_op jit(solution)/shard_map/dot_general | solution.py:14
  61.1 6.0 %fusion.4 = bf16[256,8192]{1,0:T(8,128)(2,1)S(1)} fusion(bf16[256,8192]{1,0:T(8,128)(2,1)S(1)} %fusion.3, f32[256,8192]{1,0:T(8,128)} %get-tuple-element.222, bf16[1,2,256,256]{3,2,1,0:T(8,128)(2,1)S(1)} %copy-done.6), kind=kOutput, calls=%fused_computation.15 | convolution fusion | flops 1092616192 | bytes 16908288 | tf_op jit(solution)/shard_map/dot_general | solution.py:73
  67.1 1.3 %convolution_bitcast_fusion.7 = f32[1,256,256]{2,1,0:T(8,128)S(1)} fusion(bf16[256,8192]{1,0:T(8,128)(2,1)S(1)} %copy-done.8, bf16[256,8192]{1,0:T(8,128)(2,1)S(1)} %fusion.4), kind=kOutput, calls=%fused_computation.26 | convolution fusion | flops 1073741824 | bytes 8650752 | tf_op jit(solution)/shard_map/dot_general | solution.py:14
  68.4 0.7 copy-done.11
  69.1 8.0 %fusion.7 = f32[1,32,256]{2,1,0:T(8,128)S(1)} fusion(bf16[32,8192]{1,0:T(8,128)(2,1)S(1)} %bitcast.152, bf16[256,8192]{1,0:T(8,128)(2,1)} %copy-done.11, f32[256,8192]{1,0:T(8,128)} %get-tuple-element.220, bf16[1,2,256,256]{3,2,1,0:T(8,128)(2,1)S(1)} %copy-done.6), kind=kOutput, calls=%fused_computation.27 | convolution fusion | flops 1226833920 | bytes 13271040 | tf_op jit(solution)/shard_map/dot_general | solution.py:14
  77.1 0.9 maximum_bitcast_fusion
  78.0 3.4 %convolution_bitcast_fusion.8 = f32[1,256,4]{1,2,0:T(4,128)S(1)} fusion(bf16[256,8192]{1,0:T(8,128)(2,1)} %copy-done.1, bf16[3,8192]{1,0:T(4,128)(2,1)S(1)} %get-tuple-element.212, bf16[1,8192]{1,0:T(2,128)(2,1)S(1)} %bitcast.156), kind=kOutput, calls=%fused_computation.28 | convolution fusion | flops 16908288 | bytes 4263936 | tf_op jit(solution)/shard_map/dot_general | solution.py:14
  81.4 11.1 %all-reduce = (f32[1,32,256]{2,1,0:T(8,128)}, f32[1,256,4]{1,2,0:T(4,128)}) all-reduce(f32[1,32,256]{2,1,0:T(8,128)S(1)} %fusion.7, f32[1,256,4]{1,2,0:T(4,128)S(1)} %convolution_bitcast_fusion.8), channel_id=1, replica_groups=mesh['vol'=8,'rep'=4] {'rep'}, use_global_device_ids=true, to_apply=%region_10.11 | all-reduce | flops 9216 | bytes 73728 | tf_op jit(solution)/shard_map/psum | solution.py:141
  92.5 16.3 %all-reduce.3.cloned.1.call-done = f32[1,2,256,256]{3,2,1,0:T(8,128)} async-done(((f32[1,2,256,256]{3,2,1,0:T(8,128)}), f32[1,2,256,256]{3,2,1,0:T(8,128)}) %all-reduce.3.cloned.1.call-update) | async-done | bytes 524304 | tf_op jit(solution)/shard_map/psum | solution.py:141
  108.7 1.9 %copy.43 = f32[1,2,256,256]{3,2,1,0:T(8,128)} copy(f32[1,2,256,256]{3,2,1,0:T(8,128)} %all-reduce.3.cloned.1.call-done) | data formatting | bytes 1048576
  (106 shorter events, 2.4 us)
Async XLA Ops:
  7.2 27.9 %copy-start = (s32[2048,8]{0,1:T(8,128)S(1)}, s32[2048,8]{0,1:T(8,128)}, u32[]{:S(2)}) copy-start(s32[2048,8]{0,1:T(8,128)} %param.15) | copy-start | bytes 196612
  8.6 5.5 %copy-start.6 = (bf16[1,2,256,256]{3,2,1,0:T(8,128)(2,1)S(1)}, bf16[1,2,256,256]{3,2,1,0:T(8,128)(2,1)}, u32[]{:S(2)}) copy-start(bf16[1,2,256,256]{3,2,1,0:T(8,128)(2,1)} %param.18) | copy-start | bytes 786436
  14.1 4.9 %copy-start.7 = (bf16[256,8192]{1,0:T(8,128)(2,1)}, bf16[256,8192]{1,0:T(8,128)(2,1)S(1)}, u32[]{:S(2)}) copy-start(bf16[256,8192]{1,0:T(8,128)(2,1)S(1)} %get-tuple-element.219) | copy-start | bytes 12582916
  18.9 4.9 %copy-start.9 = (bf16[256,8192]{1,0:T(8,128)(2,1)}, bf16[256,8192]{1,0:T(8,128)(2,1)S(1)}, u32[]{:S(2)}) copy-start(bf16[256,8192]{1,0:T(8,128)(2,1)S(1)} %get-tuple-element.221) | copy-start | bytes 12582916
  18.9 6.9 %copy-start.5 = (bf16[1,256,4]{1,2,0:T(4,128)(2,1)S(1)}, bf16[1,256,4]{1,2,0:T(4,128)(2,1)}, u32[]{:S(2)}) copy-start(bf16[1,256,4]{1,2,0:T(4,128)(2,1)} %param.19) | copy-start | bytes 6148
  18.9 7.7 %copy-start.2 = (f32[1,4,2048]{2,1,0:T(4,128)S(1)}, f32[1,4,2048]{2,1,0:T(4,128)}, u32[]{:S(2)}) copy-start(f32[1,4,2048]{2,1,0:T(4,128)} %param.13) | copy-start | bytes 98308
  18.9 7.7 %copy-start.3 = (s32[1,2048]{1,0:T(1,128)S(1)}, s32[1,2048]{1,0:T(1,128)}, u32[]{:S(2)}) copy-start(s32[1,2048]{1,0:T(1,128)} %param.14) | copy-start | bytes 24580
  19.0 16.1 %copy-start.4 = (f32[3,2048]{1,0:T(4,128)S(1)}, f32[3,2048]{1,0:T(4,128)}, u32[]{:S(2)}) copy-start(f32[3,2048]{1,0:T(4,128)} %param.16) | copy-start | bytes 73732
  23.8 2.0 %copy-start.1 = (bf16[256,8192]{1,0:T(8,128)(2,1)}, bf16[256,8192]{1,0:T(8,128)(2,1)S(1)}, u32[]{:S(2)}) copy-start(bf16[256,8192]{1,0:T(8,128)(2,1)S(1)} %get-tuple-element.223) | copy-start | bytes 12582916
  27.7 14.0 %all-to-all-start = ((f32[1,4,8,256]{3,1,0,2:T(4,128)}), f32[1,4,8,256]{3,1,0,2:T(4,128)S(1)}, u32[]{:S(2)}, u32[]{:S(2)}) async-start(f32[1,4,8,256]{3,1,0,2:T(4,128)} %pad_maximum_fusion.1), calls=%async_computation | async-start | bytes 65536 | tf_op jit(solution)/shard_map/all_to_all | solution.py:123
  43.4 9.9 %all-to-all-start.1 = ((f32[8,2,1,256]{3,1,2,0:T(2,128)}), f32[8,2,1,256]{3,1,2,0:T(2,128)S(1)}, u32[]{:S(2)}, u32[]{:S(2)}) async-start(f32[8,2,1,256]{3,1,2,0:T(2,128)} %maximum_bitcast_fusion.1), calls=%async_computation.1 | async-start | bytes 32768 | tf_op jit(solution)/shard_map/all_to_all | solution.py:128
  46.8 62.0 %all-reduce.3.cloned.1.call-start = ((), (), s32[]{:S(2)}) async-start(), calls=%async_computation.2 | async-start | bytes 1048576 | tf_op jit(solution)/shard_map/psum | solution.py:141
  53.9 5.8 %copy-start.10 = (bf16[256,8192]{1,0:T(8,128)(2,1)S(1)}, bf16[256,8192]{1,0:T(8,128)(2,1)}, u32[]{:S(2)}) copy-start(bf16[256,8192]{1,0:T(8,128)(2,1)} %copy-done.9) | copy-start | bytes 12582916
  61.0 6.1 %copy-start.8 = (bf16[256,8192]{1,0:T(8,128)(2,1)S(1)}, bf16[256,8192]{1,0:T(8,128)(2,1)}, u32[]{:S(2)}) copy-start(bf16[256,8192]{1,0:T(8,128)(2,1)} %copy-done.7) | copy-start | bytes 12582916
  67.1 2.0 %copy-start.11 = (bf16[256,8192]{1,0:T(8,128)(2,1)}, bf16[256,8192]{1,0:T(8,128)(2,1)S(1)}, u32[]{:S(2)}) copy-start(bf16[256,8192]{1,0:T(8,128)(2,1)S(1)} %fusion.4) | copy-start | bytes 12582916
Sparse Core Ops, SparseCore 0:
  78.1 30.5 all-reduce.2
where the time goes:
time: 118 us; the launch traced here: 117 us
  matrix products  41.7 us (35%)
  waiting for transfers between devices  29.2 us (25%)
  between operations  14.4 us (12%)
  blocking collectives  11.1 us (9%)
  starting transfers between devices  10.8 us (9%)
  local copies, waits for them, and re-layouts  6.63 us (6%)
  other arithmetic  3.04 us (3%)
    psum x1, waiting for transfers between devices, per_device(): lax.psum((first_grad, middle_grad, last_grad), 'rep')  16.3 us
    dot_general x4, matrix products, contract_first(): lax.dot_general(matrix, rows, (((0,), (0,)), ((), ())), preferred_element...  15.9 us
    dot_general x4, matrix products, contract_last(): lax.dot_general(left, right, (((1,), (1,)), ((), ())), preferred_element_...  14 us
    psum x1, blocking collectives, per_device(): lax.psum((first_grad, middle_grad, last_grad), 'rep')  11.1 us
    all_to_all x1, starting transfers between devices, per_device(): lax.all_to_all(outgoing, 'vol', split_axis=2, concat_axis=0, tiled=True)  7.28 us
    all_to_all x1, waiting for transfers between devices, per_device(): lax.all_to_all(outgoing, 'vol', split_axis=2, concat_axis=0, tiled=True)  6.62 us
    all_to_all x1, waiting for transfers between devices, per_device(): lax.all_to_all(packed, 'vol', split_axis=0, concat_axis=2, tiled=True)  6.27 us
    dot_general x1, matrix products, network_gradients(): jnp.dot(middle_weight[depth], back, preferred_element_type=jnp.float32)  6.04 us
  transfers between devices with their start and end apart: 3, of which 3 were waited for; matrix products, arithmetic and copies ran while one was open for 3% of the time, Pallas kernels for 0%

commit v1 on v0

v1 whole, which is shorter than its diff:
```python
import functools

import jax
import jax.numpy as jnp
from jax import lax
from jax.experimental import pallas as pl
from jax.experimental.pallas import tpu as pltpu
from jax.sharding import PartitionSpec as P

F32 = jnp.float32
BF16 = jnp.bfloat16
MESH = pl.DeviceIdType.MESH
HEADS = 16


def mul(left, right):
    return jnp.dot(left, right, preferred_element_type=F32)


def mul_nt(left, right):
    return lax.dot_general(left, right, (((1,), (1,)), ((), ())), preferred_element_type=F32)


def logistic(pre):
    return 0.5 * jnp.tanh(0.5 * pre) + 0.5


def activate(pre):
    gate = logistic(pre)
    hidden = pre * gate
    slope = gate + hidden * (1.0 - gate)
    return hidden.astype(BF16), slope.astype(BF16)


def kernel(
    dims,
    x_ref, deltas_ref, counts_ref, rank_ref, cot_ref,
    first_t_ref, mid_t_ref, last_t_ref, mid_ref, last_ref,
    out_ref,
    hidden, slope, gates, leaving, weights, spans, facing, seg, acc, half_in, half_x,
    seg_send, seg_recv, one_send, one_recv, two_send, two_recv, three_send, three_recv,
):
    volumes, replicas, samples, rays, depth, width, feats = dims
    chunk = rays // 4
    chunks = rays // chunk
    columns = samples * rays
    block = columns // 8
    pairs = replicas // 2
    mine = lax.axis_index("vol")
    rep = lax.axis_index("rep")
    core = lax.rem(rep, 2)
    across = rep // 2
    sibling = rep + 1 - 2 * core

    barrier = pltpu.get_barrier_semaphore()
    for k in range(1, volumes):
        pl.semaphore_signal(
            barrier, inc=1, device_id={"vol": lax.rem(mine + k, volumes)}, device_id_type=MESH
        )
    pl.semaphore_signal(barrier, inc=1, device_id={"rep": sibling}, device_id_type=MESH)
    for k in range(1, pairs):
        pl.semaphore_signal(
            barrier,
            inc=1,
            device_id={"rep": lax.rem(across + k, pairs) * 2 + core},
            device_id_type=MESH,
        )
    pl.semaphore_wait(barrier, volumes - 1 + pairs)

    def cols(start):
        return pl.ds(pl.multiple_of(start, 128), chunk)

    def seg_copy(q, k):
        part = cols(q * chunk)
        return pltpu.make_async_remote_copy(
            src_ref=seg.at[mine, :, part],
            dst_ref=seg.at[mine, :, part],
            send_sem=seg_send.at[q, k],
            recv_sem=seg_recv.at[q, k],
            device_id={"vol": lax.rem(mine + k, volumes)},
            device_id_type=MESH,
        )

    acc[...] = jnp.zeros_like(acc)

    def forward(q, carry):
        part = cols(q * chunk)
        cot = cot_ref[:, part]
        count = counts_ref[:, part]
        heads = []
        for s in range(samples):
            place = cols(s * rays + q * chunk)
            h, d = activate(mul(first_t_ref[...], x_ref[:, place]))
            hidden[0, :, place] = h
            slope[0, :, place] = d
            for k in range(depth):
                h, d = activate(mul(mid_t_ref[k], h))
                hidden[k + 1, :, place] = h
                slope[k + 1, :, place] = d
            heads.append(mul(last_t_ref[...], h)[:8])
        reached = jnp.zeros((1, chunk), F32)
        before = jnp.ones((1, chunk), F32)
        colour = jnp.zeros((1, chunk), F32)
        for s in range(samples):
            gate = logistic(heads[s])
            top = heads[s][0:1]
            density = jnp.maximum(top, 0.0) + jnp.log1p(jnp.exp(-jnp.abs(top)))
            span = jnp.where(s < count, deltas_ref[s : s + 1, part], 0.0)
            reached = reached + density * span
            after = jnp.exp(-reached)
            weight = before - after
            before = after
            face = jnp.sum(cot * gate, axis=0, keepdims=True)
            colour = colour + weight * face
            gates[s, :, part] = gate
            leaving[s : s + 1, part] = after
            weights[s : s + 1, part] = weight
            spans[s : s + 1, part] = span
            facing[s : s + 1, part] = face
        seg[mine, :, part] = jnp.concatenate([colour, -reached], axis=0)
        for k in range(1, volumes):
            seg_copy(q, k).start()
        return carry

    lax.fori_loop(0, chunks, forward, 0)

    def one(g, first, half):
        give = pl.multiple_of(first + (1 - core) * half, 8)
        return pltpu.make_async_remote_copy(
            src_ref=acc.at[pl.ds(give, half)],
            dst_ref=half_in.at[pl.ds(first // 2, half)],
            send_sem=one_send.at[g],
            recv_sem=one_recv.at[g],
            device_id={"rep": sibling},
            device_id_type=MESH,
        )

    def two(g, first, half, k):
        place = half_x.at[across, pl.ds(first // 2, half)]
        return pltpu.make_async_remote_copy(
            src_ref=place,
            dst_ref=place,
            send_sem=two_send.at[g, k],
            recv_sem=two_recv.at[g, k],
            device_id={"rep": lax.rem(across + k, pairs) * 2 + core},
            device_id_type=MESH,
        )

    def three(g, first, half):
        keep = pl.multiple_of(first + core * half, 8)
        return pltpu.make_async_remote_copy(
            src_ref=out_ref.at[pl.ds(keep, half)],
            dst_ref=out_ref.at[pl.ds(keep, half)],
            send_sem=three_send.at[g],
            recv_sem=three_recv.at[g],
            device_id={"rep": sibling},
            device_id_type=MESH,
        )

    def stage_two(g, first, half):
        one(g, first, half).wait()
        keep = pl.ds(pl.multiple_of(first + core * half, 8), half)
        half_x[across, pl.ds(first // 2, half)] = acc[keep] + half_in[pl.ds(first // 2, half)]
        for k in range(1, pairs):
            two(g, first, half, k).start()

    def stage_three(g, first, half):
        for k in range(1, pairs):
            two(g, first, half, k).wait()
        total = half_x[0, pl.ds(first // 2, half)]
        for k in range(1, pairs):
            total = total + half_x[k, pl.ds(first // 2, half)]
        out_ref[pl.ds(pl.multiple_of(first + core * half, 8), half)] = total
        three(g, first, half).start()

    groups = [(0, 0, (width + HEADS) // 2)]
    for k in range(1, depth):
        groups.append((k, groups[-1][1] + 2 * groups[-1][2], width // 2))
    groups.append((depth, groups[-1][1] + 2 * groups[-1][2], feats // 2))

    def top_layer(q, carry):
        part = cols(q * chunk)
        for k in range(1, volumes):
            seg_copy(q, k).wait()
        own_rank = rank_ref[pl.ds(mine, 1), part]
        ranks = rank_ref[:, part]
        logs = [seg[u, 1:2, part] for u in range(volumes)]
        summed = jnp.zeros(ranks.shape, F32)
        for u in range(volumes):
            summed = summed + jnp.where(ranks[u : u + 1] < ranks, logs[u], 0.0)
        prefix = jnp.exp(summed)
        behind = jnp.zeros((1, chunk), F32)
        own_log = jnp.zeros((1, chunk), F32)
        for u in range(volumes):
            term = prefix[u : u + 1] * seg[u, 0:1, part]
            behind = behind + jnp.where(ranks[u : u + 1] > own_rank, term, 0.0)
            own_log = own_log + jnp.where(ranks[u : u + 1] < own_rank, logs[u], 0.0)
        own = jnp.exp(own_log)
        cot = cot_ref[:, part] * own
        first_row = lax.broadcasted_iota(jnp.int32, (8, chunk), 0) == 0
        later = jnp.zeros((1, chunk), F32)
        outer = jnp.zeros((width, width), F32)
        outer_last = jnp.zeros((HEADS, width), F32)
        for s in reversed(range(samples)):
            place = cols(s * rays + q * chunk)
            gate = gates[s, :, part]
            weight = weights[s : s + 1, part]
            face = own * facing[s : s + 1, part]
            dopt = (face * leaving[s : s + 1, part] - later - behind) * spans[s : s + 1, part]
            later = later + face * weight
            g_head = jnp.where(first_row, dopt * gate, weight * cot * gate * (1.0 - gate))
            g_head = jnp.concatenate([g_head, jnp.zeros((HEADS - 8, chunk), F32)], axis=0).astype(BF16)
            outer_last = outer_last + mul_nt(g_head, hidden[depth, :, place])
            g = (mul(last_ref[...], g_head) * slope[depth, :, place].astype(F32)).astype(BF16)
            slope[depth, :, place] = g
            outer = outer + mul_nt(hidden[depth - 1, :, place], g)
        acc[0:width] += outer
        acc[width : width + HEADS] += outer_last
        return carry

    lax.fori_loop(0, chunks, top_layer, 0)
    one(*groups[0]).start()

    def layer(k, i):
        place = pl.ds(pl.multiple_of(i * block, 128), block)
        g = (mul(mid_ref[k], slope[k + 1, :, place]) * slope[k, :, place].astype(F32)).astype(BF16)
        if k:
            slope[k, :, place] = g
        _, first, half = groups[depth - k]
        below = hidden[k - 1, :, place] if k else x_ref[:, place]
        acc[first : first + 2 * half] += mul_nt(below, g)

    for k in reversed(range(depth)):
        at = depth - 1 - k

        @pl.loop(0, 4)
        def _(i):
            layer(k, i)

        stage_two(*groups[at])
        if at:
            stage_three(*groups[at - 1])

        @pl.loop(4, 8)
        def _(i):
            layer(k, i)

        one(*groups[at + 1]).start()
    stage_three(*groups[depth - 1])
    stage_two(*groups[depth])
    stage_three(*groups[depth])
    for group in groups:
        three(*group).wait()


def per_device(
    features, deltas, counts, order_rank, cotangent, first_weight, middle_weight, last_weight
):
    volumes = lax.axis_size("vol")
    replicas = lax.axis_size("rep")
    feats, samples, rays = features.shape[1:]
    depth, width = middle_weight.shape[1:3]
    columns = samples * rays
    x = features[0].reshape(feats, columns)
    channels = last_weight.shape[2]
    last = jnp.pad(last_weight[0], ((0, 0), (0, HEADS - channels)))
    cot = jnp.pad(cotangent, ((1, 8 - channels), (0, 0)))
    dims = (volumes, replicas, samples, rays, depth, width, feats)
    rows = depth * width + HEADS + feats
    pairs = replicas // 2
    dma = pltpu.SemaphoreType.DMA
    out = pl.pallas_call(
        functools.partial(kernel, dims),
        out_shape=jax.ShapeDtypeStruct((rows, width), F32),
        in_specs=[pl.BlockSpec(memory_space=pltpu.VMEM)] * 10,
        out_specs=pl.BlockSpec(memory_space=pltpu.VMEM),
        scratch_shapes=[
            pltpu.VMEM((depth + 1, width, columns), BF16),
            pltpu.VMEM((depth + 1, width, columns), BF16),
            pltpu.VMEM((samples, 8, rays), F32),
            pltpu.VMEM((samples, rays), F32),
            pltpu.VMEM((samples, rays), F32),
            pltpu.VMEM((samples, rays), F32),
            pltpu.VMEM((samples, rays), F32),
            pltpu.VMEM((volumes, 2, rays), F32),
            pltpu.VMEM((rows, width), F32),
            pltpu.VMEM((rows // 2, width), F32),
            pltpu.VMEM((pairs, rows // 2, width), F32),
            dma((4, volumes)),
            dma((4, volumes)),
            dma((depth + 1,)),
            dma((depth + 1,)),
            dma((depth + 1, pairs)),
            dma((depth + 1, pairs)),
            dma((depth + 1,)),
            dma((depth + 1,)),
        ],
        compiler_params=pltpu.CompilerParams(
            collective_id=0, has_side_effects=True, vmem_limit_bytes=48 * 1024 * 1024
        ),
    )(
        x,
        deltas[0],
        counts,
        order_rank.T,
        cot,
        first_weight[0].T,
        jnp.swapaxes(middle_weight[0], 1, 2),
        last.T,
        middle_weight[0],
        last,
    )
    top = width + HEADS
    middle = [out[top + (k - 1) * width : top + k * width] for k in range(depth - 1, 0, -1)]
    middle.append(out[:width])
    first_grad = out[rows - feats :]
    last_grad = out[width : width + channels].T
    return (first_grad[None], jnp.stack(middle, axis=0)[None], last_grad[None])


def solution(mesh):
    placed = (
        P("vol", None, None, "rep"),
        P("vol", None, "rep"),
        P("vol", "rep"),
        P("rep", None),
        P(None, "rep"),
        P("vol", None, None),
        P("vol", None, None, None),
        P("vol", None, None),
    )
    return jax.shard_map(
        per_device,
        mesh=mesh,
        in_specs=placed,
        out_specs=(P("vol", None, None), P("vol", None, None, None), P("vol", None, None)),
        check_vma=False,
    )
```

time: 118 us -> 48.1 us (0.41)
  Pallas kernels: 0 us -> 42.9 us
  matrix products: 41.7 us -> 0 us
  waiting for transfers between devices: 29.2 us -> 0 us
  between operations: 14.4 us -> 0.75 us
  blocking collectives: 11.1 us -> 0 us
  starting transfers between devices: 10.8 us -> 0 us
  local copies, waits for them, and re-layouts: 6.63 us -> 3.43 us
  other arithmetic: 3.04 us -> 0.83 us
    pallas_call x0 -> x1, Pallas kernels: none -> 42.9 us  [per_device(): pl.pallas_call(functools.partial(kernel, dims), out_shape=jax.ShapeDtypeS...]
    dot_general x10 -> x0, matrix products: 41.7 us -> none  [the longest x4 15.9 us: contract_first(): lax.dot_general(matrix, rows, (((0,), (0,)), ((), ())), preferred_element...]
    psum x1 -> x0, waiting for transfers between devices: 16.3 us -> none  [per_device(): lax.psum((first_grad, middle_grad, last_grad), 'rep')]
    all_to_all x2 -> x0, waiting for transfers between devices: 12.9 us -> none  [the longest x1 6.62 us: per_device(): lax.all_to_all(outgoing, 'vol', split_axis=2, concat_axis=0, tiled=True)]
    psum x1 -> x0, blocking collectives: 11.1 us -> none  [per_device(): lax.psum((first_grad, middle_grad, last_grad), 'rep')]
    all_to_all x2 -> x0, starting transfers between devices: 10.6 us -> none  [the longest x1 7.28 us: per_device(): lax.all_to_all(outgoing, 'vol', split_axis=2, concat_axis=0, tiled=True)]
    unnamed x31 -> x17, local copies, waits for them, and re-layouts: 6.03 us -> 1.1 us
    broadcast_in_dim x0 -> x2, local copies, waits for them, and re-layouts: none -> 1.21 us  [per_device(): return (first_grad[None], jnp.stack(middle, axis=0)[None], last_grad[None])]
  transfers between devices with their start and end apart: 3 -> 0, of which waited for: 3 -> 0; matrix products, arithmetic and copies ran while one was open for 3% -> 0% of each run, Pallas kernels for 0% -> 0%
where the time goes in v1:
time: 48.1 us; the launch traced here: 48 us
  Pallas kernels  42.9 us (89%)
  local copies, waits for them, and re-layouts  3.43 us (7%)
  other arithmetic  0.83 us (2%)
  between operations  0.75 us (2%)
    pallas_call x1, Pallas kernels, per_device(): pl.pallas_call(functools.partial(kernel, dims), out_shape=jax.ShapeDtypeS...  42.9 us
    broadcast_in_dim x2, local copies, waits for them, and re-layouts, per_device(): return (first_grad[None], jnp.stack(middle, axis=0)[None], last_grad[None])  1.21 us
    unnamed x17, local copies, waits for them, and re-layouts  1.1 us

profile of v1, /device:TPU:0, one launch (start us, length us, event | category | flops | bytes accessed | tf_op | source)
XLA Modules:
  0.0 48.0 jit_solution(1194211998980272750)
XLA Ops:
  0.6 0.0 copy-start.5
  0.6 0.0 copy-start.6
  0.7 0.0 copy-start
  0.7 0.0 copy-start.4
  0.7 0.8 %pad.8.cot_ref = f32[8,2048]{1,0:T(8,128)S(1)} pad(f32[3,2048]{1,0:T(4,128)} %param.12, f32[]{:T(128)} %constant.3.clone.1), padding=1_4x0_0 | pad | bytes 90116 | tf_op jit(solution)/shard_map/jit(_pad)/pad | solution.py:267
  1.5 0.0 copy-done.5
  1.5 0.1 copy.11
  1.6 0.0 copy-done.6
  1.7 0.1 copy.12
  1.8 0.1 copy.14.last_t_ref
  1.9 0.0 copy-done
  1.9 0.2 copy.13.mid_t_ref
  2.1 0.0 copy-done.4
  2.1 0.0 copy-start.1
  2.1 0.0 copy-start.2
  2.1 0.0 copy-start.3
  2.1 0.3 copy.15
  2.4 0.5 %copy-done.1 = s32[2048,8]{0,1:T(8,128)S(1)} copy-done((s32[2048,8]{0,1:T(8,128)S(1)}, s32[2048,8]{0,1:T(8,128)}, u32[]{:S(2)}) %copy-start.1) | copy-done | bytes 65560
  2.9 0.0 copy-done.2
  2.9 0.0 copy-done.3
  2.9 42.9 %shard_map.103 = f32[560,256]{1,0:T(8,128)S(1)} custom-call(bf16[32,8192]{1,0:T(8,128)(2,1)S(1)} %bitcast.26, f32[4,2048]{1,0:T(4,128)S(1)} %bitcast.31, s32[1,2048]{1,0:T(1,128)S(1)} %copy-done.3, s32[8,2048]{1,0:T(8,128)S(1)} %bitcast.30, f32[8,2048]{1,0:T(8,128)S(1)} %pad.8.cot_ref, bf16[256,32]{1,0:T(8,128)(2,1)S(1)} %bitcast.29, ...), custom_call_target="tpu_custom_call" | custom-call | tf_op jit(solution)/shard_map/pallas_call | solution.py:272
  45.9 0.6 %slice_bitcast_fusion.3 = f32[1,256,4]{1,2,0:T(4,128)} fusion(f32[560,256]{1,0:T(8,128)S(1)} %shard_map.103), kind=kLoop, calls=%fused_computation.4 | loop fusion | bytes 8192 | tf_op jit(solution)/shard_map/broadcast_in_dim | solution.py:318
  46.5 0.6 %slice_bitcast_fusion.2 = f32[1,32,256]{2,1,0:T(8,128)} fusion(f32[560,256]{1,0:T(8,128)S(1)} %shard_map.103), kind=kLoop, calls=%fused_computation.3 | loop fusion | bytes 65536 | tf_op jit(solution)/shard_map/broadcast_in_dim | solution.py:318
  47.1 0.8 %maximum_bitcast_fusion = f32[1,2,256,256]{3,2,1,0:T(8,128)} fusion(f32[1,256,256]{2,1,0:T(8,128)S(1)} %get-tuple-element.4, f32[1,256,256]{2,1,0:T(8,128)S(1)} %get-tuple-element.3), kind=kLoop, calls=%fused_computation | loop fusion | flops 131072 | bytes 1048576 | tf_op jit(solution)/shard_map/broadcast_in_dim | solution.py:318
  (2 shorter events, 0.1 us)
Async XLA Ops:
  0.6 0.9 %copy-start.5 = (bf16[1,32,256]{2,1,0:T(8,128)(2,1)S(1)}, bf16[1,32,256]{2,1,0:T(8,128)(2,1)}, u32[]{:S(2)}) copy-start(bf16[1,32,256]{2,1,0:T(8,128)(2,1)} %param.13) | copy-start | bytes 49156
  0.6 1.0 %copy-start.6 = (bf16[1,256,4]{1,2,0:T(4,128)(2,1)S(1)}, bf16[1,256,4]{1,2,0:T(4,128)(2,1)}, u32[]{:S(2)}) copy-start(bf16[1,256,4]{1,2,0:T(4,128)(2,1)} %param.15) | copy-start | bytes 6148
  0.7 1.2 %copy-start = (bf16[1,2,256,256]{3,2,1,0:T(8,128)(2,1)S(1)}, bf16[1,2,256,256]{3,2,1,0:T(8,128)(2,1)}, u32[]{:S(2)}) copy-start(bf16[1,2,256,256]{3,2,1,0:T(8,128)(2,1)} %param.14) | copy-start | bytes 786436
  0.7 1.4 %copy-start.4 = (bf16[1,32,4,2048]{3,2,1,0:T(4,128)(2,1)S(1)}, bf16[1,32,4,2048]{3,2,1,0:T(4,128)(2,1)}, u32[]{:S(2)}) copy-start(bf16[1,32,4,2048]{3,2,1,0:T(4,128)(2,1)} %param.8) | copy-start | bytes 1572868
  2.1 0.8 %copy-start.1 = (s32[2048,8]{0,1:T(8,128)S(1)}, s32[2048,8]{0,1:T(8,128)}, u32[]{:S(2)}) copy-start(s32[2048,8]{0,1:T(8,128)} %param.11) | copy-start | bytes 196612
  2.1 0.8 %copy-start.2 = (f32[1,4,2048]{2,1,0:T(4,128)S(1)}, f32[1,4,2048]{2,1,0:T(4,128)}, u32[]{:S(2)}) copy-start(f32[1,4,2048]{2,1,0:T(4,128)} %param.9) | copy-start | bytes 98308
  2.1 0.8 %copy-start.3 = (s32[1,2048]{1,0:T(1,128)S(1)}, s32[1,2048]{1,0:T(1,128)}, u32[]{:S(2)}) copy-start(s32[1,2048]{1,0:T(1,128)} %counts_ref.1) | copy-start | bytes 24580

commit v2 on v1

--- a/solution.py
+++ b/solution.py
@@ -25,10 +25,10 @@
     return 0.5 * jnp.tanh(0.5 * pre) + 0.5
 
 
-def activate(pre):
-    gate = logistic(pre)
-    hidden = pre * gate
-    slope = gate + hidden * (1.0 - gate)
+def activate(half):
+    twice = jnp.tanh(half) + 1.0
+    hidden = half * twice
+    slope = twice + hidden * (2.0 - twice)
     return hidden.astype(BF16), slope.astype(BF16)
 
 
@@ -36,7 +36,7 @@
     dims,
     x_ref, deltas_ref, counts_ref, rank_ref, cot_ref,
     first_t_ref, mid_t_ref, last_t_ref, mid_ref, last_ref,
-    out_ref,
+    middle_ref, small_ref,
     hidden, slope, gates, leaving, weights, spans, facing, seg, acc, half_in, half_x,
     seg_send, seg_recv, one_send, one_recv, two_send, two_recv, three_send, three_recv,
 ):
@@ -65,8 +65,6 @@
             device_id={"rep": lax.rem(across + k, pairs) * 2 + core},
             device_id_type=MESH,
         )
-    pl.semaphore_wait(barrier, volumes - 1 + pairs)
-
     def cols(start):
         return pl.ds(pl.multiple_of(start, 128), chunk)
 
@@ -81,23 +79,28 @@
             device_id_type=MESH,
         )
 
+    def padded(cot):
+        below = jnp.zeros((7 - cot.shape[0], cot.shape[1]), F32)
+        return jnp.concatenate([jnp.zeros((1, cot.shape[1]), F32), cot, below], axis=0)
+
     acc[...] = jnp.zeros_like(acc)
 
     def forward(q, carry):
         part = cols(q * chunk)
-        cot = cot_ref[:, part]
+        cot = padded(cot_ref[:, part])
         count = counts_ref[:, part]
-        heads = []
-        for s in range(samples):
-            place = cols(s * rays + q * chunk)
-            h, d = activate(mul(first_t_ref[...], x_ref[:, place]))
-            hidden[0, :, place] = h
-            slope[0, :, place] = d
-            for k in range(depth):
-                h, d = activate(mul(mid_t_ref[k], h))
-                hidden[k + 1, :, place] = h
-                slope[k + 1, :, place] = d
-            heads.append(mul(last_t_ref[...], h)[:8])
+        places = [cols(s * rays + q * chunk) for s in range(samples)]
+        below = [x_ref[:, place] for place in places]
+        for k in range(depth + 1):
+            matrix = mid_t_ref[k - 1] if k else first_t_ref[...]
+            above = []
+            for s, place in enumerate(places):
+                h, d = activate(mul(matrix, below[s]))
+                hidden[k, :, place] = h
+                slope[k, :, place] = d
+                above.append(h)
+            below = above
+        heads = [mul(last_t_ref[...], h)[:8] for h in below]
         reached = jnp.zeros((1, chunk), F32)
         before = jnp.ones((1, chunk), F32)
         colour = jnp.zeros((1, chunk), F32)
@@ -118,6 +121,11 @@
             spans[s : s + 1, part] = span
             facing[s : s + 1, part] = face
         seg[mine, :, part] = jnp.concatenate([colour, -reached], axis=0)
+
+        @pl.when(q == 0)
+        def _():
+            pl.semaphore_wait(barrier, volumes - 1 + pairs)
+
         for k in range(1, volumes):
             seg_copy(q, k).start()
         return carry
@@ -146,11 +154,14 @@
             device_id_type=MESH,
         )
 
+    def landing(g, half):
+        rows = pl.ds(pl.multiple_of(core * half, 8), half)
+        return small_ref.at[rows] if g == depth else middle_ref.at[depth - 1 - g, rows]
+
     def three(g, first, half):
-        keep = pl.multiple_of(first + core * half, 8)
         return pltpu.make_async_remote_copy(
-            src_ref=out_ref.at[pl.ds(keep, half)],
-            dst_ref=out_ref.at[pl.ds(keep, half)],
+            src_ref=landing(g, half),
+            dst_ref=landing(g, half),
             send_sem=three_send.at[g],
             recv_sem=three_recv.at[g],
             device_id={"rep": sibling},
@@ -170,13 +181,11 @@
         total = half_x[0, pl.ds(first // 2, half)]
         for k in range(1, pairs):
             total = total + half_x[k, pl.ds(first // 2, half)]
-        out_ref[pl.ds(pl.multiple_of(first + core * half, 8), half)] = total
+        landing(g, half)[...] = total
         three(g, first, half).start()
 
-    groups = [(0, 0, (width + HEADS) // 2)]
-    for k in range(1, depth):
-        groups.append((k, groups[-1][1] + 2 * groups[-1][2], width // 2))
-    groups.append((depth, groups[-1][1] + 2 * groups[-1][2], feats // 2))
+    groups = [(k, k * width, width // 2) for k in range(depth)]
+    groups.append((depth, depth * width, (feats + HEADS) // 2))
 
     def top_layer(q, carry):
         part = cols(q * chunk)
@@ -196,7 +205,7 @@
             behind = behind + jnp.where(ranks[u : u + 1] > own_rank, term, 0.0)
             own_log = own_log + jnp.where(ranks[u : u + 1] < own_rank, logs[u], 0.0)
         own = jnp.exp(own_log)
-        cot = cot_ref[:, part] * own
+        cot = padded(cot_ref[:, part]) * own
         first_row = lax.broadcasted_iota(jnp.int32, (8, chunk), 0) == 0
         later = jnp.zeros((1, chunk), F32)
         outer = jnp.zeros((width, width), F32)
@@ -215,7 +224,7 @@
             slope[depth, :, place] = g
             outer = outer + mul_nt(hidden[depth - 1, :, place], g)
         acc[0:width] += outer
-        acc[width : width + HEADS] += outer_last
+        acc[depth * width + feats :] += outer_last
         return carry
 
     lax.fori_loop(0, chunks, top_layer, 0)
@@ -226,9 +235,9 @@
         g = (mul(mid_ref[k], slope[k + 1, :, place]) * slope[k, :, place].astype(F32)).astype(BF16)
         if k:
             slope[k, :, place] = g
-        _, first, half = groups[depth - k]
+        first = (depth - k) * width
         below = hidden[k - 1, :, place] if k else x_ref[:, place]
-        acc[first : first + 2 * half] += mul_nt(below, g)
+        acc[first : first + below.shape[0]] += mul_nt(below, g)
 
     for k in reversed(range(depth)):
         at = depth - 1 - k
@@ -264,16 +273,20 @@
     x = features[0].reshape(feats, columns)
     channels = last_weight.shape[2]
     last = jnp.pad(last_weight[0], ((0, 0), (0, HEADS - channels)))
-    cot = jnp.pad(cotangent, ((1, 8 - channels), (0, 0)))
+    half = jnp.asarray(0.5, BF16)
+    middle = middle_weight[0] * half
     dims = (volumes, replicas, samples, rays, depth, width, feats)
     rows = depth * width + HEADS + feats
     pairs = replicas // 2
     dma = pltpu.SemaphoreType.DMA
-    out = pl.pallas_call(
+    middle_grad, small = pl.pallas_call(
         functools.partial(kernel, dims),
-        out_shape=jax.ShapeDtypeStruct((rows, width), F32),
+        out_shape=(
+            jax.ShapeDtypeStruct((depth, width, width), F32),
+            jax.ShapeDtypeStruct((feats + HEADS, width), F32),
+        ),
         in_specs=[pl.BlockSpec(memory_space=pltpu.VMEM)] * 10,
-        out_specs=pl.BlockSpec(memory_space=pltpu.VMEM),
+        out_specs=(pl.BlockSpec(memory_space=pltpu.VMEM),) * 2,
         scratch_shapes=[
             pltpu.VMEM((depth + 1, width, columns), BF16),
             pltpu.VMEM((depth + 1, width, columns), BF16),
@@ -303,19 +316,16 @@
         deltas[0],
         counts,
         order_rank.T,
-        cot,
-        first_weight[0].T,
-        jnp.swapaxes(middle_weight[0], 1, 2),
+        cotangent,
+        first_weight[0].T * half,
+        jnp.swapaxes(middle, 1, 2),
         last.T,
-        middle_weight[0],
-        last,
+        middle,
+        last * half,
     )
-    top = width + HEADS
-    middle = [out[top + (k - 1) * width : top + k * width] for k in range(depth - 1, 0, -1)]
-    middle.append(out[:width])
-    first_grad = out[rows - feats :]
-    last_grad = out[width : width + channels].T
-    return (first_grad[None], jnp.stack(middle, axis=0)[None], last_grad[None])
+    first_grad = small[:feats]
+    last_grad = small[feats : feats + channels].T
+    return (first_grad[None], middle_grad[None], last_grad[None])
 
 
 def solution(mesh):

time: 48.1 us -> 40.8 us (0.85)
  Pallas kernels: 42.9 us -> 34.2 us
  local copies, waits for them, and re-layouts: 3.43 us -> 5.56 us
  other arithmetic: 0.83 us -> 0.07 us
    pallas_call x1, Pallas kernels: 42.9 us -> 34.2 us  [per_device(): pl.pallas_call(functools.partial(kernel, dims), out_shape=(jax.ShapeDtype...]
    unnamed x17 -> x16, local copies, waits for them, and re-layouts: 1.1 us -> 4.15 us
    pad x2 -> x0, local copies, waits for them, and re-layouts: 0.87 us -> none  [the longest x1 0.84 us: per_device(): cot = jnp.pad(cotangent, ((1, 8 - channels), (0, 0)))]
    broadcast_in_dim x1 -> x0, other arithmetic: 0.83 us -> none  [per_device(): return (first_grad[None], jnp.stack(middle, axis=0)[None], last_grad[None])]
where the time goes in v2:
time: 40.8 us; the launch traced here: 40.5 us
  Pallas kernels  34.2 us (84%)
  local copies, waits for them, and re-layouts  5.56 us (14%)
  between operations  0.71 us (2%)
    pallas_call x1, Pallas kernels, per_device(): pl.pallas_call(functools.partial(kernel, dims), out_shape=(jax.ShapeDtype...  34.2 us
    unnamed x16, local copies, waits for them, and re-layouts  4.15 us
    broadcast_in_dim x2, local copies, waits for them, and re-layouts, per_device(): return (first_grad[None], middle_grad[None], last_grad[None])  1.21 us

profile of v2, /device:TPU:0, one launch (start us, length us, event | category | flops | bytes accessed | tf_op | source)
XLA Modules:
  0.0 40.5 jit_solution(6268647121986456000)
XLA Ops:
  0.6 0.0 copy-start.4
  0.6 0.9 %copy.11 = bf16[1,32,256]{1,2,0:T(8,128)(2,1)S(1)} copy(bf16[1,32,256]{2,1,0:T(8,128)(2,1)} %param.13) | data formatting | bytes 32768 | tf_op args[5]
  1.5 0.8 %copy.12 = bf16[1,256,4]{2,1,0:T(8,128)(2,1)S(1)} copy(bf16[1,256,4]{1,2,0:T(4,128)(2,1)} %param.15) | data formatting | bytes 4096 | tf_op args[7]
  2.4 0.1 copy.14.last_t_ref
  2.5 0.0 copy-done.4
  2.5 0.0 copy-start.5
  2.5 0.3 copy.15
  2.8 0.7 %copy-done.5 = bf16[1,2,256,256]{3,2,1,0:T(8,128)(2,1)S(1)} copy-done((bf16[1,2,256,256]{3,2,1,0:T(8,128)(2,1)S(1)}, bf16[1,2,256,256]{3,2,1,0:T(8,128)(2,1)}, u32[]{:S(2)}) %copy-start.5) | copy-done | bytes 262168
  3.5 0.0 copy-start
  3.5 0.0 copy-start.1
  3.5 0.0 copy-start.2
  3.5 0.0 copy-start.3
  3.5 0.1 copy.13.mid_t_ref
  3.7 0.7 %copy-done = s32[2048,8]{0,1:T(8,128)S(1)} copy-done((s32[2048,8]{0,1:T(8,128)S(1)}, s32[2048,8]{0,1:T(8,128)}, u32[]{:S(2)}) %copy-start) | copy-done | bytes 65560
  4.3 0.0 copy-done.1
  4.3 0.0 copy-done.2
  4.3 0.0 copy-done.3
  4.3 34.2 %shard_map.103 = (f32[2,256,256]{2,1,0:T(8,128)S(1)}, f32[48,256]{1,0:T(8,128)S(1)}) custom-call(bf16[32,8192]{1,0:T(8,128)(2,1)S(1)} %bitcast.24, f32[4,2048]{1,0:T(4,128)S(1)} %bitcast.27, s32[1,2048]{1,0:T(1,128)S(1)} %copy-done.3, s32[8,2048]{1,0:T(8,128)S(1)} %bitcast.26, f32[3,2048]{1,0:T(4,128)S(1)} %copy-done.2, ...), custom_call_target="tpu_custom_call" | custom-call | tf_op jit(solution)/shard_map/pallas_call | solution.py:282
  38.5 0.6 %slice_bitcast_fusion.1 = f32[1,256,4]{1,2,0:T(4,128)} fusion(f32[48,256]{1,0:T(8,128)S(1)} %get-tuple-element.5), kind=kLoop, calls=%fused_computation.6 | loop fusion | bytes 8192 | tf_op jit(solution)/shard_map/broadcast_in_dim | solution.py:328
  39.1 0.6 %slice_bitcast_fusion = f32[1,32,256]{2,1,0:T(8,128)} fusion(f32[48,256]{1,0:T(8,128)S(1)} %get-tuple-element.5), kind=kLoop, calls=%fused_computation.5 | loop fusion | bytes 65536 | tf_op jit(solution)/shard_map/broadcast_in_dim | solution.py:328
  39.7 0.8 %copy.17 = f32[1,2,256,256]{3,2,1,0:T(8,128)} copy(f32[1,2,256,256]{3,2,1,0:T(8,128)S(1)} %bitcast.25) | data formatting | bytes 1048576
  (3 shorter events, 0.1 us)
Async XLA Ops:
  0.6 1.8 %copy-start.4 = (bf16[1,32,4,2048]{3,2,1,0:T(4,128)(2,1)S(1)}, bf16[1,32,4,2048]{3,2,1,0:T(4,128)(2,1)}, u32[]{:S(2)}) copy-start(bf16[1,32,4,2048]{3,2,1,0:T(4,128)(2,1)} %param.8) | copy-start | bytes 1572868
  2.5 1.0 %copy-start.5 = (bf16[1,2,256,256]{3,2,1,0:T(8,128)(2,1)S(1)}, bf16[1,2,256,256]{3,2,1,0:T(8,128)(2,1)}, u32[]{:S(2)}) copy-start(bf16[1,2,256,256]{3,2,1,0:T(8,128)(2,1)} %param.14) | copy-start | bytes 786436
  3.5 0.8 %copy-start = (s32[2048,8]{0,1:T(8,128)S(1)}, s32[2048,8]{0,1:T(8,128)}, u32[]{:S(2)}) copy-start(s32[2048,8]{0,1:T(8,128)} %param.11) | copy-start | bytes 196612
  3.5 0.8 %copy-start.1 = (f32[1,4,2048]{2,1,0:T(4,128)S(1)}, f32[1,4,2048]{2,1,0:T(4,128)}, u32[]{:S(2)}) copy-start(f32[1,4,2048]{2,1,0:T(4,128)} %param.9) | copy-start | bytes 98308
  3.5 0.8 %copy-start.2 = (f32[3,2048]{1,0:T(4,128)S(1)}, f32[3,2048]{1,0:T(4,128)}, u32[]{:S(2)}) copy-start(f32[3,2048]{1,0:T(4,128)} %cot_ref.1) | copy-start | bytes 73732
  3.5 0.8 %copy-start.3 = (s32[1,2048]{1,0:T(1,128)S(1)}, s32[1,2048]{1,0:T(1,128)}, u32[]{:S(2)}) copy-start(s32[1,2048]{1,0:T(1,128)} %counts_ref.1) | copy-start | bytes 24580

commit v3 on v2

--- a/solution.py
+++ b/solution.py
@@ -37,8 +37,8 @@
     x_ref, deltas_ref, counts_ref, rank_ref, cot_ref,
     first_t_ref, mid_t_ref, last_t_ref, mid_ref, last_ref,
     middle_ref, small_ref,
-    hidden, slope, gates, leaving, weights, spans, facing, seg, acc, half_in, half_x,
-    seg_send, seg_recv, one_send, one_recv, two_send, two_recv, three_send, three_recv,
+    hidden, slope, gates, leaving, weights, spans, facing, seg, acc, half_in, half_x, small_in,
+    seg_send, seg_recv, one_send, one_recv, two_send, two_recv, three_send, three_recv, all_send, all_recv,
 ):
     volumes, replicas, samples, rays, depth, width, feats = dims
     chunk = rays // 4
@@ -57,14 +57,11 @@
         pl.semaphore_signal(
             barrier, inc=1, device_id={"vol": lax.rem(mine + k, volumes)}, device_id_type=MESH
         )
-    pl.semaphore_signal(barrier, inc=1, device_id={"rep": sibling}, device_id_type=MESH)
-    for k in range(1, pairs):
+    for k in range(1, replicas):
         pl.semaphore_signal(
-            barrier,
-            inc=1,
-            device_id={"rep": lax.rem(across + k, pairs) * 2 + core},
-            device_id_type=MESH,
-        )
+            barrier, inc=1, device_id={"rep": lax.rem(rep + k, replicas)}, device_id_type=MESH
+        )
+
     def cols(start):
         return pl.ds(pl.multiple_of(start, 128), chunk)
 
@@ -124,7 +121,7 @@
 
         @pl.when(q == 0)
         def _():
-            pl.semaphore_wait(barrier, volumes - 1 + pairs)
+            pl.semaphore_wait(barrier, volumes - 1 + replicas - 1)
 
         for k in range(1, volumes):
             seg_copy(q, k).start()
@@ -156,7 +153,7 @@
 
     def landing(g, half):
         rows = pl.ds(pl.multiple_of(core * half, 8), half)
-        return small_ref.at[rows] if g == depth else middle_ref.at[depth - 1 - g, rows]
+        return middle_ref.at[depth - 1 - g, rows]
 
     def three(g, first, half):
         return pltpu.make_async_remote_copy(
@@ -185,7 +182,35 @@
         three(g, first, half).start()
 
     groups = [(k, k * width, width // 2) for k in range(depth)]
-    groups.append((depth, depth * width, (feats + HEADS) // 2))
+    pieces = [(feats, HEADS), (0, feats)]
+
+    def whole(p, k):
+        first, count = pieces[p]
+        return pltpu.make_async_remote_copy(
+            src_ref=acc.at[pl.ds(depth * width + first, count)],
+            dst_ref=small_in.at[rep, pl.ds(first, count)],
+            send_sem=all_send.at[p, k],
+            recv_sem=all_recv.at[p, k],
+            device_id={"rep": lax.rem(rep + k, replicas)},
+            device_id_type=MESH,
+        )
+
+    def push(p):
+        for k in range(1, replicas):
+            whole(p, k).start()
+        first, count = pieces[p]
+        rows = pl.ds(first, count)
+        small_in[rep, rows] = acc[pl.ds(depth * width + first, count)]
+
+    def collect(p):
+        for k in range(1, replicas):
+            whole(p, k).wait()
+        first, count = pieces[p]
+        rows = pl.ds(first, count)
+        total = small_in[0, rows]
+        for j in range(1, replicas):
+            total = total + small_in[j, rows]
+        small_ref[rows] = total
 
     def top_layer(q, carry):
         part = cols(q * chunk)
@@ -229,6 +254,7 @@
 
     lax.fori_loop(0, chunks, top_layer, 0)
     one(*groups[0]).start()
+    push(0)
 
     def layer(k, i):
         place = pl.ds(pl.multiple_of(i * block, 128), block)
@@ -242,7 +268,7 @@
     for k in reversed(range(depth)):
         at = depth - 1 - k
 
-        @pl.loop(0, 4)
+        @pl.loop(0, 2)
         def _(i):
             layer(k, i)
 
@@ -250,14 +276,16 @@
         if at:
             stage_three(*groups[at - 1])
 
-        @pl.loop(4, 8)
+        @pl.loop(2, 8)
         def _(i):
             layer(k, i)
 
-        one(*groups[at + 1]).start()
+        if k:
+            one(*groups[at + 1]).start()
+    push(1)
     stage_three(*groups[depth - 1])
-    stage_two(*groups[depth])
-    stage_three(*groups[depth])
+    collect(0)
+    collect(1)
     for group in groups:
         three(*group).wait()
 
@@ -297,16 +325,19 @@
             pltpu.VMEM((samples, rays), F32),
             pltpu.VMEM((volumes, 2, rays), F32),
             pltpu.VMEM((rows, width), F32),
-            pltpu.VMEM((rows // 2, width), F32),
-            pltpu.VMEM((pairs, rows // 2, width), F32),
+            pltpu.VMEM((depth * width // 2, width), F32),
+            pltpu.VMEM((pairs, depth * width // 2, width), F32),
+            pltpu.VMEM((replicas, feats + HEADS, width), F32),
             dma((4, volumes)),
             dma((4, volumes)),
-            dma((depth + 1,)),
-            dma((depth + 1,)),
-            dma((depth + 1, pairs)),
-            dma((depth + 1, pairs)),
-            dma((depth + 1,)),
-            dma((depth + 1,)),
+            dma((depth,)),
+            dma((depth,)),
+            dma((depth, pairs)),
+            dma((depth, pairs)),
+            dma((depth,)),
+            dma((depth,)),
+            dma((2, replicas)),
+            dma((2, replicas)),
         ],
         compiler_params=pltpu.CompilerParams(
             collective_id=0, has_side_effects=True, vmem_limit_bytes=48 * 1024 * 1024

time: 40.8 us -> 38.8 us (0.951)
  Pallas kernels: 34.2 us -> 32.2 us
    pallas_call x1, Pallas kernels: 34.2 us -> 32.2 us  [per_device(): pl.pallas_call(functools.partial(kernel, dims), out_shape=(jax.ShapeDtype...]
where the time goes in v3:
time: 38.8 us; the launch traced here: 38.6 us
  Pallas kernels  32.2 us (83%)
  local copies, waits for them, and re-layouts  5.56 us (14%)
  between operations  0.71 us (2%)
    pallas_call x1, Pallas kernels, per_device(): pl.pallas_call(functools.partial(kernel, dims), out_shape=(jax.ShapeDtype...  32.2 us
    unnamed x16, local copies, waits for them, and re-layouts  4.15 us
    broadcast_in_dim x2, local copies, waits for them, and re-layouts, per_device(): return (first_grad[None], middle_grad[None], last_grad[None])  1.21 us

profile of v3, /device:TPU:0, one launch (start us, length us, event | category | flops | bytes accessed | tf_op | source)
XLA Modules:
  0.0 38.6 jit_solution(7132389365274393871)
XLA Ops:
  0.6 0.0 copy-start.4
  0.6 0.9 %copy.11 = bf16[1,32,256]{1,2,0:T(8,128)(2,1)S(1)} copy(bf16[1,32,256]{2,1,0:T(8,128)(2,1)} %param.13) | data formatting | bytes 32768 | tf_op args[5]
  1.5 0.8 %copy.12 = bf16[1,256,4]{2,1,0:T(8,128)(2,1)S(1)} copy(bf16[1,256,4]{1,2,0:T(4,128)(2,1)} %param.15) | data formatting | bytes 4096 | tf_op args[7]
  2.4 0.1 copy.14.last_t_ref
  2.5 0.0 copy-done.4
  2.5 0.0 copy-start.5
  2.5 0.3 copy.15
  2.8 0.7 %copy-done.5 = bf16[1,2,256,256]{3,2,1,0:T(8,128)(2,1)S(1)} copy-done((bf16[1,2,256,256]{3,2,1,0:T(8,128)(2,1)S(1)}, bf16[1,2,256,256]{3,2,1,0:T(8,128)(2,1)}, u32[]{:S(2)}) %copy-start.5) | copy-done | bytes 262168
  3.5 0.0 copy-start
  3.5 0.0 copy-start.1
  3.5 0.0 copy-start.2
  3.5 0.0 copy-start.3
  3.5 0.1 copy.13.mid_t_ref
  3.7 0.7 %copy-done = s32[2048,8]{0,1:T(8,128)S(1)} copy-done((s32[2048,8]{0,1:T(8,128)S(1)}, s32[2048,8]{0,1:T(8,128)}, u32[]{:S(2)}) %copy-start) | copy-done | bytes 65560
  4.3 0.0 copy-done.1
  4.3 0.0 copy-done.2
  4.3 0.0 copy-done.3
  4.3 32.2 %shard_map.103 = (f32[2,256,256]{2,1,0:T(8,128)S(1)}, f32[48,256]{1,0:T(8,128)S(1)}) custom-call(bf16[32,8192]{1,0:T(8,128)(2,1)S(1)} %bitcast.24, f32[4,2048]{1,0:T(4,128)S(1)} %bitcast.27, s32[1,2048]{1,0:T(1,128)S(1)} %copy-done.3, s32[8,2048]{1,0:T(8,128)S(1)} %bitcast.26, f32[3,2048]{1,0:T(4,128)S(1)} %copy-done.2, ...), custom_call_target="tpu_custom_call" | custom-call | tf_op jit(solution)/shard_map/pallas_call | solution.py:310
  36.5 0.6 %slice_bitcast_fusion.1 = f32[1,256,4]{1,2,0:T(4,128)} fusion(f32[48,256]{1,0:T(8,128)S(1)} %get-tuple-element.5), kind=kLoop, calls=%fused_computation.6 | loop fusion | bytes 8192 | tf_op jit(solution)/shard_map/broadcast_in_dim | solution.py:359
  37.1 0.6 %slice_bitcast_fusion = f32[1,32,256]{2,1,0:T(8,128)} fusion(f32[48,256]{1,0:T(8,128)S(1)} %get-tuple-element.5), kind=kLoop, calls=%fused_computation.5 | loop fusion | bytes 65536 | tf_op jit(solution)/shard_map/broadcast_in_dim | solution.py:359
  37.8 0.8 %copy.17 = f32[1,2,256,256]{3,2,1,0:T(8,128)} copy(f32[1,2,256,256]{3,2,1,0:T(8,128)S(1)} %bitcast.25) | data formatting | bytes 1048576
  (3 shorter events, 0.1 us)
Async XLA Ops:
  0.6 1.8 %copy-start.4 = (bf16[1,32,4,2048]{3,2,1,0:T(4,128)(2,1)S(1)}, bf16[1,32,4,2048]{3,2,1,0:T(4,128)(2,1)}, u32[]{:S(2)}) copy-start(bf16[1,32,4,2048]{3,2,1,0:T(4,128)(2,1)} %param.8) | copy-start | bytes 1572868
  2.5 1.0 %copy-start.5 = (bf16[1,2,256,256]{3,2,1,0:T(8,128)(2,1)S(1)}, bf16[1,2,256,256]{3,2,1,0:T(8,128)(2,1)}, u32[]{:S(2)}) copy-start(bf16[1,2,256,256]{3,2,1,0:T(8,128)(2,1)} %param.14) | copy-start | bytes 786436
  3.5 0.8 %copy-start = (s32[2048,8]{0,1:T(8,128)S(1)}, s32[2048,8]{0,1:T(8,128)}, u32[]{:S(2)}) copy-start(s32[2048,8]{0,1:T(8,128)} %param.11) | copy-start | bytes 196612
  3.5 0.8 %copy-start.1 = (f32[1,4,2048]{2,1,0:T(4,128)S(1)}, f32[1,4,2048]{2,1,0:T(4,128)}, u32[]{:S(2)}) copy-start(f32[1,4,2048]{2,1,0:T(4,128)} %param.9) | copy-start | bytes 98308
  3.5 0.8 %copy-start.2 = (f32[3,2048]{1,0:T(4,128)S(1)}, f32[3,2048]{1,0:T(4,128)}, u32[]{:S(2)}) copy-start(f32[3,2048]{1,0:T(4,128)} %cot_ref.1) | copy-start | bytes 73732
  3.5 0.8 %copy-start.3 = (s32[1,2048]{1,0:T(1,128)S(1)}, s32[1,2048]{1,0:T(1,128)}, u32[]{:S(2)}) copy-start(s32[1,2048]{1,0:T(1,128)} %counts_ref.1) | copy-start | bytes 24580

commit v4 on v3

--- a/solution.py
+++ b/solution.py
@@ -44,7 +44,7 @@
     chunk = rays // 4
     chunks = rays // chunk
     columns = samples * rays
-    block = columns // 8
+    block = columns // 4
     pairs = replicas // 2
     mine = lax.axis_index("vol")
     rep = lax.axis_index("rep")
@@ -268,7 +268,7 @@
     for k in reversed(range(depth)):
         at = depth - 1 - k
 
-        @pl.loop(0, 2)
+        @pl.loop(0, 1)
         def _(i):
             layer(k, i)
 
@@ -276,7 +276,7 @@
         if at:
             stage_three(*groups[at - 1])
 
-        @pl.loop(2, 8)
+        @pl.loop(1, 4)
         def _(i):
             layer(k, i)
 

time: 38.8 us -> 37.2 us (0.959)
  Pallas kernels: 32.2 us -> 30.6 us
    pallas_call x1, Pallas kernels: 32.2 us -> 30.6 us  [per_device(): pl.pallas_call(functools.partial(kernel, dims), out_shape=(jax.ShapeDtype...]
where the time goes in v4:
time: 37.2 us; the launch traced here: 36.9 us
  Pallas kernels  30.6 us (82%)
  local copies, waits for them, and re-layouts  5.56 us (15%)
  between operations  0.71 us (2%)
    pallas_call x1, Pallas kernels, per_device(): pl.pallas_call(functools.partial(kernel, dims), out_shape=(jax.ShapeDtype...  30.6 us
    unnamed x16, local copies, waits for them, and re-layouts  4.15 us
    broadcast_in_dim x2, local copies, waits for them, and re-layouts, per_device(): return (first_grad[None], middle_grad[None], last_grad[None])  1.21 us

profile of v4, /device:TPU:0, one launch (start us, length us, event | category | flops | bytes accessed | tf_op | source)
XLA Modules:
  0.0 36.9 jit_solution(12698184014825473329)
XLA Ops:
  0.6 0.0 copy-start.4
  0.6 0.9 %copy.11 = bf16[1,32,256]{1,2,0:T(8,128)(2,1)S(1)} copy(bf16[1,32,256]{2,1,0:T(8,128)(2,1)} %param.13) | data formatting | bytes 32768 | tf_op args[5]
  1.5 0.8 %copy.12 = bf16[1,256,4]{2,1,0:T(8,128)(2,1)S(1)} copy(bf16[1,256,4]{1,2,0:T(4,128)(2,1)} %param.15) | data formatting | bytes 4096 | tf_op args[7]
  2.4 0.1 copy.14.last_t_ref
  2.5 0.0 copy-done.4
  2.5 0.0 copy-start.5
  2.5 0.3 copy.15
  2.8 0.7 %copy-done.5 = bf16[1,2,256,256]{3,2,1,0:T(8,128)(2,1)S(1)} copy-done((bf16[1,2,256,256]{3,2,1,0:T(8,128)(2,1)S(1)}, bf16[1,2,256,256]{3,2,1,0:T(8,128)(2,1)}, u32[]{:S(2)}) %copy-start.5) | copy-done | bytes 262168
  3.5 0.0 copy-start
  3.5 0.0 copy-start.1
  3.5 0.0 copy-start.2
  3.5 0.0 copy-start.3
  3.5 0.1 copy.13.mid_t_ref
  3.7 0.7 %copy-done = s32[2048,8]{0,1:T(8,128)S(1)} copy-done((s32[2048,8]{0,1:T(8,128)S(1)}, s32[2048,8]{0,1:T(8,128)}, u32[]{:S(2)}) %copy-start) | copy-done | bytes 65560
  4.3 0.0 copy-done.1
  4.3 0.0 copy-done.2
  4.3 0.0 copy-done.3
  4.3 30.6 %shard_map.103 = (f32[2,256,256]{2,1,0:T(8,128)S(1)}, f32[48,256]{1,0:T(8,128)S(1)}) custom-call(bf16[32,8192]{1,0:T(8,128)(2,1)S(1)} %bitcast.24, f32[4,2048]{1,0:T(4,128)S(1)} %bitcast.27, s32[1,2048]{1,0:T(1,128)S(1)} %copy-done.3, s32[8,2048]{1,0:T(8,128)S(1)} %bitcast.26, f32[3,2048]{1,0:T(4,128)S(1)} %copy-done.2, ...), custom_call_target="tpu_custom_call" | custom-call | tf_op jit(solution)/shard_map/pallas_call | solution.py:310
  34.9 0.6 %slice_bitcast_fusion.1 = f32[1,256,4]{1,2,0:T(4,128)} fusion(f32[48,256]{1,0:T(8,128)S(1)} %get-tuple-element.5), kind=kLoop, calls=%fused_computation.6 | loop fusion | bytes 8192 | tf_op jit(solution)/shard_map/broadcast_in_dim | solution.py:359
  35.5 0.6 %slice_bitcast_fusion = f32[1,32,256]{2,1,0:T(8,128)} fusion(f32[48,256]{1,0:T(8,128)S(1)} %get-tuple-element.5), kind=kLoop, calls=%fused_computation.5 | loop fusion | bytes 65536 | tf_op jit(solution)/shard_map/broadcast_in_dim | solution.py:359
  36.1 0.8 %copy.17 = f32[1,2,256,256]{3,2,1,0:T(8,128)} copy(f32[1,2,256,256]{3,2,1,0:T(8,128)S(1)} %bitcast.25) | data formatting | bytes 1048576
  (3 shorter events, 0.1 us)
Async XLA Ops:
  0.6 1.8 %copy-start.4 = (bf16[1,32,4,2048]{3,2,1,0:T(4,128)(2,1)S(1)}, bf16[1,32,4,2048]{3,2,1,0:T(4,128)(2,1)}, u32[]{:S(2)}) copy-start(bf16[1,32,4,2048]{3,2,1,0:T(4,128)(2,1)} %param.8) | copy-start | bytes 1572868
  2.5 1.0 %copy-start.5 = (bf16[1,2,256,256]{3,2,1,0:T(8,128)(2,1)S(1)}, bf16[1,2,256,256]{3,2,1,0:T(8,128)(2,1)}, u32[]{:S(2)}) copy-start(bf16[1,2,256,256]{3,2,1,0:T(8,128)(2,1)} %param.14) | copy-start | bytes 786436
  3.5 0.8 %copy-start = (s32[2048,8]{0,1:T(8,128)S(1)}, s32[2048,8]{0,1:T(8,128)}, u32[]{:S(2)}) copy-start(s32[2048,8]{0,1:T(8,128)} %param.11) | copy-start | bytes 196612
  3.5 0.8 %copy-start.1 = (f32[1,4,2048]{2,1,0:T(4,128)S(1)}, f32[1,4,2048]{2,1,0:T(4,128)}, u32[]{:S(2)}) copy-start(f32[1,4,2048]{2,1,0:T(4,128)} %param.9) | copy-start | bytes 98308
  3.5 0.8 %copy-start.2 = (f32[3,2048]{1,0:T(4,128)S(1)}, f32[3,2048]{1,0:T(4,128)}, u32[]{:S(2)}) copy-start(f32[3,2048]{1,0:T(4,128)} %cot_ref.1) | copy-start | bytes 73732
  3.5 0.8 %copy-start.3 = (s32[1,2048]{1,0:T(1,128)S(1)}, s32[1,2048]{1,0:T(1,128)}, u32[]{:S(2)}) copy-start(s32[1,2048]{1,0:T(1,128)} %counts_ref.1) | copy-start | bytes 24580
